TPU v7x, 32 devices: a whole 2x2x4 slice. The times are simulated.
32 devices in a mesh: cand: 8 (over z, y), tp: 4 (over x, core).
Axes of the slice: x: 2, y: 2, z: 4, core: 2. Of those that a mesh axis runs over, the one named last changes fastest.
Arguments:
- reward_query: bfloat16 [64, 32, 8192], P('cand', None, 'tp'), may hold values from -170 to 170
- reward_new: bfloat16 [64, 2, 32, 1024], P('cand', None, None, 'tp'), may hold values from -7 to 7
- reward_key_value_cache: bfloat16 [64, 2, 768, 1024], P('cand', None, None, 'tp'), may hold values from -6 to 6
- reward_length: int32 [64], P('cand'), may hold values from 1 to 768
- out_weight: bfloat16 [8192, 4096], P('tp'), may hold values from -0.09375 to 0.09375
- policy_cache: bfloat16 [64, 2, 768, 1024], P('cand', None, None, 'tp'), may hold values from -6 to 6
- policy_length: int32 [64], replicated, may hold values from 1 to 767
- source: int32 [32], replicated, may hold values from 0 to 63, as said below
- policy_query: bfloat16 [32, 8192], P('cand', 'tp'), may hold values from -170 to 170
- policy_new: bfloat16 [32, 2, 1024], P('cand', None, 'tp'), may hold values from -7 to 7
Outputs:
- reward_out: bfloat16 [2048, 4096], P('cand', 'tp')
- compacted: bfloat16 [32, 2, 768, 1024], P('cand', None, None, 'tp')
- policy_attn: bfloat16 [32, 8192], P('cand', 'tp')
Inputs may be any that keep to these rules, and one draw needn't show every extreme that they name: `source`: distinct candidate indices; the 8 candidates of each index of cand are named exactly 4 times.
All inputs are finite; a program needn't handle non-finite values.
Results may differ from a plain program's by a relative error of at most 0.0057.
Values may be sent and summed in bfloat16 or wider, within the bound.
No kernel may reach another device: no remote copies, remote signals or barrier semaphores. Data moves between devices by JAX's collectives and lax.ppermute only.
A program may use at most 128 MiB of HBM per device.

v0:
```python
import jax
import jax.numpy as jnp
from jax import lax
from jax.sharding import PartitionSpec as P

ASKING_UNITS = 64
SHARED_KV_UNITS = 8
ATTN_DIM = 128
NEW_TOKEN_COUNT = 32
CACHE_LENGTH = 768


def body(
    reward_query,
    reward_new,
    reward_key_value_cache,
    reward_length,
    out_weight,
    policy_cache,
    policy_length,
    source,
    policy_query,
    policy_new,
):
    attention_clusters = ASKING_UNITS // SHARED_KV_UNITS
    score_scale = ATTN_DIM ** (-0.5)
    count = reward_query.shape[0]
    kv_heads = reward_key_value_cache.shape[-1] // ATTN_DIM
    head_list = reward_query.reshape(count, NEW_TOKEN_COUNT, kv_heads, attention_clusters, ATTN_DIM)
    cache_keys = reward_key_value_cache[:, 0].reshape(count, CACHE_LENGTH, kv_heads, ATTN_DIM)
    cache_values = reward_key_value_cache[:, 1].reshape(count, CACHE_LENGTH, kv_heads, ATTN_DIM)
    fresh_keys = reward_new[:, 0].reshape(count, NEW_TOKEN_COUNT, kv_heads, ATTN_DIM)
    fresh_values = reward_new[:, 1].reshape(count, NEW_TOKEN_COUNT, kv_heads, ATTN_DIM)
    old_scores = (
        jnp.einsum("ctkgd,cpkd->ckgtp", head_list, cache_keys, preferred_element_type=jnp.float32)
        * score_scale
    )
    new_scores = (
        jnp.einsum("ctkgd,cukd->ckgtu", head_list, fresh_keys, preferred_element_type=jnp.float32)
        * score_scale
    )
    cache_rows = lax.iota(jnp.int32, CACHE_LENGTH)
    old_visible = cache_rows[None, :] < reward_length[:, None]
    old_scores = jnp.where(old_visible[:, None, None, None, :], old_scores, -1e30)
    token_rows = lax.iota(jnp.int32, NEW_TOKEN_COUNT)
    new_visible = token_rows[None, :] <= token_rows[:, None]
    new_scores = jnp.where(new_visible, new_scores, -1e30)
    peak = jnp.maximum(old_scores.max(-1), new_scores.max(-1))[..., None]
    old_exp = jnp.exp(old_scores - peak)
    new_exp = jnp.exp(new_scores - peak)
    denominator = old_exp.sum(-1, keepdims=True) + new_exp.sum(-1, keepdims=True)
    old_weights = (old_exp / denominator).astype(jnp.bfloat16)
    new_weights = (new_exp / denominator).astype(jnp.bfloat16)
    mixed = jnp.einsum(
        "ckgtp,cpkd->ctkgd", old_weights, cache_values, preferred_element_type=jnp.float32
    )
    mixed = mixed + jnp.einsum(
        "ckgtu,cukd->ctkgd", new_weights, fresh_values, preferred_element_type=jnp.float32
    )
    attn_rows = mixed.reshape(
        count * NEW_TOKEN_COUNT, kv_heads * attention_clusters * ATTN_DIM
    ).astype(jnp.bfloat16)
    partial_value = jnp.dot(attn_rows, out_weight, preferred_element_type=jnp.float32)
    reward_out = lax.psum_scatter(partial_value, "tp", scatter_dimension=1, tiled=True).astype(
        jnp.bfloat16
    )
    slot_count = policy_query.shape[0]
    spread = lax.all_to_all(policy_cache, "cand", split_axis=2, concat_axis=0, tiled=True)
    selected = jnp.take(spread, source, axis=0)
    moved = lax.all_to_all(selected, "cand", split_axis=0, concat_axis=2, tiled=True)
    local_source = lax.dynamic_slice_in_dim(source, lax.axis_index("cand") * slot_count, slot_count)
    slot_lengths = jnp.take(policy_length, local_source)
    compacted = jnp.where(
        cache_rows[None, None, :, None] == slot_lengths[:, None, None, None],
        policy_new[:, :, None, :],
        moved,
    )
    slot_heads = policy_query.reshape(slot_count, kv_heads, attention_clusters, ATTN_DIM)
    slot_keys = compacted[:, 0].reshape(slot_count, CACHE_LENGTH, kv_heads, ATTN_DIM)
    slot_values = compacted[:, 1].reshape(slot_count, CACHE_LENGTH, kv_heads, ATTN_DIM)
    slot_scores = (
        jnp.einsum("skgd,spkd->skgp", slot_heads, slot_keys, preferred_element_type=jnp.float32)
        * score_scale
    )
    slot_visible = cache_rows[None, :] <= slot_lengths[:, None]
    slot_scores = jnp.where(slot_visible[:, None, None, :], slot_scores, -1e30)
    slot_weights = jax.nn.softmax(slot_scores, axis=-1).astype(jnp.bfloat16)
    policy_attn = jnp.einsum(
        "skgp,spkd->skgd", slot_weights, slot_values, preferred_element_type=jnp.float32
    )
    policy_attn = policy_attn.reshape(slot_count, kv_heads * attention_clusters * ATTN_DIM).astype(
        jnp.bfloat16
    )
    return (reward_out, compacted, policy_attn)


def solution(mesh):
    in_specs = (
        P("cand", None, "tp"),
        P("cand", None, None, "tp"),
        P("cand", None, None, "tp"),
        P("cand"),
        P("tp", None),
        P("cand", None, None, "tp"),
        P(),
        P(),
        P("cand", "tp"),
        P("cand", None, "tp"),
    )
    out_specs = (P("cand", "tp"), P("cand", None, None, "tp"), P("cand", "tp"))
    return jax.shard_map(body, mesh=mesh, in_specs=in_specs, out_specs=out_specs, check_vma=False)
```

profile of v0, /device:TPU:0, one launch (start us, length us, event | category | flops | bytes accessed | tf_op | source)
XLA Modules:
  0.0 265.2 jit_solution(11354631515065026288)
XLA Ops:
  7.2 0.0 copy-start
  7.2 9.0 %copy.74 = bf16[8,2,768,256]{3,0,1,2:T(8,128)(2,1)} copy(bf16[8,2,768,256]{3,2,1,0:T(8,128)(2,1)} %param.15) | data formatting | bytes 12582912 | tf_op args[5]
  16.2 7.3 %all-to-all-start = ((bf16[8,2,768,256]{3,0,1,2:T(8,128)(2,1)}), bf16[8,2,768,256]{3,0,1,2:T(8,128)(2,1)}, u32[]{:S(2)}, u32[]{:S(2)}) async-start(bf16[8,2,768,256]{3,0,1,2:T(8,128)(2,1)} %copy.74), calls=%async_computation.1 | async-start | bytes 12582912 | tf_op jit(solution)/shard_map/all_to_all | solution.py:68
  23.5 0.2 reduce-scatter.2.cloned.1.call-start
  23.7 5.0 %fusion.22 = (bf16[8,1,768,256]{3,2,1,0:T(8,128)(2,1)}, bf16[8,1,768,256]{3,2,1,0:T(8,128)(2,1)S(1)}) fusion(bf16[8,2,768,256]{3,2,1,0:T(8,128)(2,1)} %param.12), kind=kLoop, calls=%fused_computation.48 | loop fusion | bytes 12582912 | tf_op jit(solution)/shard_map/slice | solution.py:30
  28.7 2.8 %copy.99 = bf16[8,1,768,256]{2,3,0,1:T(8,128)(2,1)} copy(bf16[8,1,768,256]{3,2,1,0:T(8,128)(2,1)S(1)} %get-tuple-element.7) | data formatting | bytes 6291456
  31.5 3.2 %copy.98 = bf16[8,1,768,256]{2,3,0,1:T(8,128)(2,1)S(1)} copy(bf16[8,1,768,256]{3,2,1,0:T(8,128)(2,1)} %get-tuple-element.6) | data formatting | bytes 6291456
  34.7 0.0 copy-start.7
  34.7 2.4 copy.100
  37.2 1.0 fusion.24
  38.2 0.0 copy-start.2
  38.3 0.0 copy-done.7
  38.3 0.1 iota_compare_fusion
  38.4 3.1 %fusion.25 = (f32[8,2,8,32]{3,2,1,0:T(8,128)S(1)}, f32[8,2,8,32,32]{3,4,2,1,0:T(8,128)S(1)}) fusion(bf16[8,32,2,8,128]{4,3,2,1,0:T(8,128)(2,1)} %bitcast.71, bf16[8,32,2,128,1]{3,2,1,0,4:T(2,128)(2,1)S(1)} %bitcast.77, pred[32,32]{0,1:T(8,128)(4,1)S(1)} %iota_compare_fusion.1), kind=kOutput, calls=%fused_computation.51 | convolution fusion | flops 33943552 | bytes 1721344 | tf_op jit(solution)/shard_map/ctkgd,cukd->ckgtu/dot_general | solution.py:39
  41.5 2.3 bitcast_reduce_fusion
  43.7 0.6 fusion.4
  44.4 3.5 %fusion.2 = f32[8,2,8,32]{3,2,1,0:T(8,128)S(1)} fusion(f32[8,2,768,32,8]{2,3,4,1,0:T(8,128)S(1)} %get-tuple-element.15, f32[8,2,8,32]{3,2,1,0:T(8,128)S(1)} %max.9, pred[8,768]{1,0:T(8,128)(4,1)S(1)} %iota_compare_fusion), kind=kLoop, calls=%fused_computation.8 | loop fusion | flops 12578816 | bytes 12621824 | tf_op jit(solution)/shard_map/reduce_sum | solution.py:51
  47.9 5.0 %fusion.3 = f32[8,2,8,32,128]{4,3,2,1,0:T(8,128)S(1)} fusion(bf16[8,768,2,128,1]{1,3,4,2,0:T(8,128)(2,1)S(1)} %bitcast.74, f32[8,2,768,32,8]{2,3,4,1,0:T(8,128)S(1)} %get-tuple-element.15, f32[8,2,8,32]{3,2,1,0:T(8,128)S(1)} %add.29, f32[8,2,8,32]{3,2,1,0:T(8,128)S(1)} %max.9, pred[8,768]{1,0:T(8,128)(4,1)S(1)} %iota_compare_fusion), kind=kOutput, calls=%fused_computation.9 | convolution fusion | flops 821035008 | bytes 17864704 | tf_op jit(solution)/shard_map/ckgtp,cpkd->ctkgd/dot_general | solution.py:54
  52.9 0.7 fusion.5
  53.6 0.4 copy.73
  54.0 0.5 convert_element_type.31
  54.5 10.1 %fusion.27 = f32[256,4096]{1,0:T(8,128)} fusion(bf16[256,2048]{1,0:T(8,128)(2,1)S(1)} %convert_element_type.31, bf16[2048,4096]{1,0:T(8,128)(2,1)} %param.14), kind=kOutput, calls=%fused_computation.53 | convolution fusion | flops 4294967296 | bytes 22020096 | tf_op jit(solution)/shard_map/dot_general | solution.py:63
  64.7 0.0 reduce-scatter.2.cloned.1.call-update
  64.7 0.6 copy-done.6
  65.4 96.3 %all-to-all-done = bf16[8,2,768,256]{3,0,1,2:T(8,128)(2,1)} async-done(((bf16[8,2,768,256]{3,0,1,2:T(8,128)(2,1)}), bf16[8,2,768,256]{3,0,1,2:T(8,128)(2,1)}, u32[]{:S(2)}, u32[]{:S(2)}) %all-to-all-start) | async-done | bytes 6291488 | tf_op jit(solution)/shard_map/all_to_all | solution.py:68
  161.7 8.0 %copy.76 = bf16[8,8,2,96,256]{4,3,2,1,0:T(8,128)(2,1)} copy(bf16[8,8,2,96,256]{4,1,2,3,0:T(8,128)(2,1)} %bitcast.11) | data formatting | bytes 12582912 | tf_op jit(solution)/shard_map/all_to_all | solution.py:68
  169.6 3.5 %gather_fusion.1 = bf16[32,2,96,256]{3,2,1,0:T(8,128)(2,1)S(1)} fusion(bf16[64,2,96,256]{3,2,1,0:T(8,128)(2,1)} %bitcast.68, s32[1024]{0:T(1024)S(1)} %pad_clamp_fusion), kind=kCustom, calls=%fused_computation.1 | custom fusion | bytes 6291584 | tf_op jit(solution)/shard_map/jit(_take)/gather | solution.py:69
  173.2 2.0 broadcast_select_fusion
  175.2 3.7 %all-to-all-start.1 = ((bf16[32,2,96,256]{3,2,1,0:T(8,128)(2,1)}), bf16[32,2,96,256]{3,2,1,0:T(8,128)(2,1)S(1)}, u32[]{:S(2)}, u32[]{:S(2)}) async-start(bf16[32,2,96,256]{3,2,1,0:T(8,128)(2,1)} %broadcast_select_fusion), calls=%async_computation.2 | async-start | bytes 6291456 | tf_op jit(solution)/shard_map/all_to_all | solution.py:70
  178.9 0.1 compare_select_fusion.1
  179.0 0.6 gather_fusion
  179.6 0.1 and_select_fusion
  179.7 0.1 iota_compare_fusion.2
  179.8 0.0 reduce-scatter.2.cloned.1.call-done
  179.8 2.1 convert_element_type.32
  181.9 67.9 %all-to-all-done.1 = bf16[32,2,96,256]{3,2,1,0:T(8,128)(2,1)S(1)} async-done(((bf16[32,2,96,256]{3,2,1,0:T(8,128)(2,1)}), bf16[32,2,96,256]{3,2,1,0:T(8,128)(2,1)S(1)}, u32[]{:S(2)}, u32[]{:S(2)}) %all-to-all-start.1) | async-done | bytes 3145760 | tf_op jit(solution)/shard_map/all_to_all | solution.py:70
  249.8 0.3 copy.77
  250.0 0.4 copy-done.5
  250.4 0.8 bitcast_select_fusion
  251.3 0.0 copy-start.1
  251.3 0.2 fusion.23
  251.5 1.4 copy-done.1
  252.9 1.6 copy.80
  254.5 0.7 copy.78
  255.2 0.3 fusion.9
  255.5 0.2 fusion.26
  255.7 2.0 fusion.10
  257.7 0.6 copy.122
  (17 shorter events, 0.1 us)
Async XLA Ops:
  7.2 171.8 %copy-start = (s32[64]{0:T(128)S(1)}, s32[64]{0:T(128)}, u32[]{:S(2)}) copy-start(s32[64]{0:T(128)} %param.16) | copy-start | bytes 772
  16.2 145.5 %all-to-all-start = ((bf16[8,2,768,256]{3,0,1,2:T(8,128)(2,1)}), bf16[8,2,768,256]{3,0,1,2:T(8,128)(2,1)}, u32[]{:S(2)}, u32[]{:S(2)}) async-start(bf16[8,2,768,256]{3,0,1,2:T(8,128)(2,1)} %copy.74), calls=%async_computation.1 | async-start | bytes 12582912 | tf_op jit(solution)/shard_map/all_to_all | solution.py:68
  23.5 156.3 %reduce-scatter.2.cloned.1.call-start = ((), (), s32[]{:S(2)}) async-start(), calls=%async_computation.3 | async-start | bytes 5242880 | tf_op jit(solution)/shard_map/reduce_scatter | solution.py:64
  34.7 3.5 %copy-start.7 = (s32[8]{0:T(128)S(1)}, s32[8]{0:T(128)}, u32[]{:S(2)}) copy-start(s32[8]{0:T(128)} %param.13) | copy-start | bytes 100
  38.2 3.2 %copy-start.2 = (bf16[32,8,16,128]{3,2,1,0:T(8,128)(2,1)S(1)}, bf16[32,8,16,128]{3,2,1,0:T(8,128)(2,1)}, u32[]{:S(2)}) copy-start(bf16[32,8,16,128]{3,2,1,0:T(8,128)(2,1)} %copy.100) | copy-start | bytes 3145732
  44.4 3.5 %copy-start.3 = (bf16[8,1,768,256]{2,3,0,1:T(8,128)(2,1)S(1)}, bf16[8,1,768,256]{2,3,0,1:T(8,128)(2,1)}, u32[]{:S(2)}) copy-start(bf16[8,1,768,256]{2,3,0,1:T(8,128)(2,1)} %copy.99) | copy-start | bytes 9437188
  64.7 0.7 copy-start.6
  175.2 74.5 %all-to-all-start.1 = ((bf16[32,2,96,256]{3,2,1,0:T(8,128)(2,1)}), bf16[32,2,96,256]{3,2,1,0:T(8,128)(2,1)S(1)}, u32[]{:S(2)}, u32[]{:S(2)}) async-start(bf16[32,2,96,256]{3,2,1,0:T(8,128)(2,1)} %broadcast_select_fusion), calls=%async_computation.2 | async-start | bytes 6291456 | tf_op jit(solution)/shard_map/all_to_all | solution.py:70
  249.7 0.7 copy-start.5
  251.3 1.7 copy-start.1
  252.9 2.3 copy-start.4
Sparse Core Ops, SparseCore 0:
  64.8 45.6 reduce-scatter.1
where the time goes:
time: 266 us; the launch traced here: 265 us
  waiting for transfers between devices  164 us (62%)
  local copies, waits for them, and re-layouts  42.5 us (16%)
  matrix products  23.5 us (9%)
  between operations  14.3 us (5%)
  starting transfers between devices  11.1 us (4%)
  other arithmetic  9.63 us (4%)
    all_to_all x1, waiting for transfers between devices, body(): lax.all_to_all(policy_cache, 'cand', split_axis=2, concat_axis=0, tiled=T...  96.3 us
    all_to_all x1, waiting for transfers between devices, body(): lax.all_to_all(selected, 'cand', split_axis=0, concat_axis=2, tiled=True)  67.9 us
    unnamed x21, local copies, waits for them, and re-layouts  20.6 us
    dot_general x1, matrix products, body(): jnp.dot(attn_rows, out_weight, preferred_element_type=jnp.float32)  10.1 us
    all_to_all x1, local copies, waits for them, and re-layouts, body(): lax.all_to_all(policy_cache, 'cand', split_axis=2, concat_axis=0, tiled=T...  7.95 us
    all_to_all x1, starting transfers between devices, body(): lax.all_to_all(policy_cache, 'cand', split_axis=2, concat_axis=0, tiled=T...  7.28 us
  transfers between devices with their start and end apart: 3, of which 2 were waited for; matrix products, arithmetic and copies ran while one was open for 22% of the time, Pallas kernels for 0%

commit v1 on v0

--- a/solution.py
+++ b/solution.py
@@ -65,8 +65,18 @@
         jnp.bfloat16
     )
     slot_count = policy_query.shape[0]
-    spread = lax.all_to_all(policy_cache, "cand", split_axis=2, concat_axis=0, tiled=True)
-    selected = jnp.take(spread, source, axis=0)
+    per_index = policy_cache.shape[0]
+    owner = source // per_index
+    slots = lax.iota(jnp.int32, source.shape[0])
+    earlier = (owner[:, None] == owner[None, :]) & (slots[None, :] < slots[:, None])
+    rank = jnp.sum(earlier.astype(jnp.int32), axis=1)
+    me = lax.axis_index("cand")
+    lane = lax.iota(jnp.int32, slot_count)
+    mine = (owner[None, :] == me) & (rank[None, :] == lane[:, None])
+    named = jnp.sum(jnp.where(mine, source[None, :] - me * per_index, 0), axis=1)
+    picked = jnp.take(policy_cache, named, axis=0)
+    spread = lax.all_to_all(picked, "cand", split_axis=2, concat_axis=0, tiled=True)
+    selected = jnp.take(spread, owner * slot_count + rank, axis=0)
     moved = lax.all_to_all(selected, "cand", split_axis=0, concat_axis=2, tiled=True)
     local_source = lax.dynamic_slice_in_dim(source, lax.axis_index("cand") * slot_count, slot_count)
     slot_lengths = jnp.take(policy_length, local_source)

time: 266 us -> 196 us (0.74)
  waiting for transfers between devices: 164 us -> 94.5 us
  local copies, waits for them, and re-layouts: 42.5 us -> 37.9 us
    all_to_all x1, waiting for transfers between devices: 96.3 us -> 26.6 us  [body(): lax.all_to_all(picked, 'cand', split_axis=2, concat_axis=0, tiled=True)]
    unnamed x21 -> x28, local copies, waits for them, and re-layouts: 20.6 us -> 12 us
    select_n x0 -> x1, local copies, waits for them, and re-layouts: none -> 4.9 us  [body(): picked = jnp.take(policy_cache, named, axis=0)]
    reduce_scatter x1, waiting for transfers between devices: 0.01 us -> 4.75 us  [body(): lax.psum_scatter(partial_value, 'tp', scatter_dimension=1, tiled=True)]
    all_to_all x1, waiting for transfers between devices: 67.9 us -> 63.1 us  [body(): lax.all_to_all(selected, 'cand', split_axis=0, concat_axis=2, tiled=True)]
    all_to_all x1 -> x2, local copies, waits for them, and re-layouts: 7.95 us -> 4.45 us  [body(): lax.all_to_all(picked, 'cand', split_axis=2, concat_axis=0, tiled=True)]
    gather x1 -> x2, local copies, waits for them, and re-layouts: 3.53 us -> 6.17 us  [the longest x1 3.53 us: body(): picked = jnp.take(policy_cache, named, axis=0)]
  transfers between devices with their start and end apart: 3 -> 3, of which waited for: 2 -> 3; matrix products, arithmetic and copies ran while one was open for 22% -> 28% of each run, Pallas kernels for 0% -> 0%
where the time goes in v1:
time: 196 us; the launch traced here: 195 us
  waiting for transfers between devices  94.5 us (48%)
  local copies, waits for them, and re-layouts  37.9 us (19%)
  matrix products  25.8 us (13%)
  between operations  14.3 us (7%)
  other arithmetic  11.6 us (6%)
  starting transfers between devices  11.3 us (6%)
    all_to_all x1, waiting for transfers between devices, body(): lax.all_to_all(selected, 'cand', split_axis=0, concat_axis=2, tiled=True)  63.1 us
    all_to_all x1, waiting for transfers between devices, body(): lax.all_to_all(picked, 'cand', split_axis=2, concat_axis=0, tiled=True)  26.6 us
    unnamed x28, local copies, waits for them, and re-layouts  12 us
    dot_general x1, matrix products, body(): jnp.dot(attn_rows, out_weight, preferred_element_type=jnp.float32)  10.1 us
    all_to_all x1, starting transfers between devices, body(): lax.all_to_all(picked, 'cand', split_axis=2, concat_axis=0, tiled=True)  7.28 us
    dot_general x1, matrix products, body(): jnp.einsum('ckgtp,cpkd->ctkgd', old_weights, cache_values, preferred_elem...  7.27 us
    slice x1, local copies, waits for them, and re-layouts, body(): reward_key_value_cache[:, 0]  5.02 us
    select_n x1, local copies, waits for them, and re-layouts, body(): picked = jnp.take(policy_cache, named, axis=0)  4.9 us
  transfers between devices with their start and end apart: 3, of which 3 were waited for; matrix products, arithmetic and copies ran while one was open for 28% of the time, Pallas kernels for 0%

profile of v1, /device:TPU:0, one launch (start us, length us, event | category | flops | bytes accessed | tf_op | source)
XLA Modules:
  0.0 195.4 jit_solution(5957872202642696703)
XLA Ops:
  7.2 0.7 broadcast_compare_fusion
  7.9 0.7 broadcast_subtract_fusion
  8.5 0.2 convert_reduce_fusion
  8.7 0.1 select_reduce_fusion
  8.9 0.4 copy-done.9
  9.2 3.5 %gather_fusion.1 = bf16[4,2,768,256]{3,2,1,0:T(8,128)(2,1)S(1)} fusion(bf16[8,2,768,256]{3,2,1,0:T(8,128)(2,1)} %param.15, s32[1024]{0:T(1024)S(1)} %pad_clamp_fusion.1), kind=kCustom, calls=%fused_computation.1 | custom fusion | bytes 6291472 | tf_op jit(solution)/shard_map/jit(_take)/gather | solution.py:77
  12.8 0.4 broadcast_select_fusion
  13.1 4.9 %copy.91 = bf16[4,2,768,256]{3,1,0,2:T(2,128)(2,1)} copy(bf16[4,2,768,256]{3,2,1,0:T(8,128)(2,1)S(1)} %broadcast_select_fusion) | data formatting | bytes 6291456 | tf_op jit(solution)/shard_map/jit(_take)/select_n | solution.py:77
  18.0 7.3 %all-to-all-start = ((bf16[4,2,768,256]{3,1,0,2:T(2,128)(2,1)}), bf16[4,2,768,256]{3,1,0,2:T(2,128)(2,1)}, u32[]{:S(2)}, u32[]{:S(2)}) async-start(bf16[4,2,768,256]{3,1,0,2:T(2,128)(2,1)} %copy.91), calls=%async_computation.1 | async-start | bytes 6291456 | tf_op jit(solution)/shard_map/all_to_all | solution.py:78
  25.3 0.2 reduce-scatter.2.cloned.1.call-start
  25.6 5.0 %fusion.25 = (bf16[8,1,768,256]{3,2,1,0:T(8,128)(2,1)}, bf16[8,1,768,256]{3,2,1,0:T(8,128)(2,1)S(1)}) fusion(bf16[8,2,768,256]{3,2,1,0:T(8,128)(2,1)} %param.12), kind=kLoop, calls=%fused_computation.67 | loop fusion | bytes 12582912 | tf_op jit(solution)/shard_map/slice | solution.py:30
  30.6 2.8 %copy.115 = bf16[8,1,768,256]{2,3,0,1:T(8,128)(2,1)} copy(bf16[8,1,768,256]{3,2,1,0:T(8,128)(2,1)S(1)} %get-tuple-element.11) | data formatting | bytes 6291456
  33.5 3.2 %copy.114 = bf16[8,1,768,256]{2,3,0,1:T(8,128)(2,1)S(1)} copy(bf16[8,1,768,256]{3,2,1,0:T(8,128)(2,1)} %get-tuple-element.10) | data formatting | bytes 6291456
  36.7 2.4 %copy.116 = bf16[32,8,16,128]{3,2,1,0:T(8,128)(2,1)} copy(bf16[32,8,16,128]{3,1,2,0:T(8,128)(2,1)} %bitcast.81) | data formatting | bytes 2097152
  39.1 1.0 fusion.27
  40.1 3.7 %bitcast_reduce_fusion = (f32[8,2,8,32]{3,2,1,0:T(8,128)S(1)}, f32[8,2,768,32,8]{2,3,4,1,0:T(8,128)S(1)}) fusion(pred[8,768]{1,0:T(8,128)(4,1)S(1)} %iota_compare_fusion, bf16[8,768,2,128,1]{1,3,4,2,0:T(8,128)(2,1)S(1)} %bitcast.72, bf16[8,32,2,8,128]{4,3,2,1,0:T(8,128)(2,1)} %bitcast.76), kind=kOutput, calls=%fused_computation.5 | convolution fusion | flops 814739456 | bytes 16799744 | tf_op jit(solution)/shard_map/ctkgd,cpkd->ckgtp/dot_general | solution.py:35
  43.8 1.8 fusion.28
  45.6 3.5 %fusion.2 = f32[8,2,8,32]{3,2,1,0:T(8,128)S(1)} fusion(f32[8,2,768,32,8]{2,3,4,1,0:T(8,128)S(1)} %get-tuple-element.19, f32[8,2,8,32]{3,2,1,0:T(8,128)S(1)} %max.9, pred[8,768]{1,0:T(8,128)(4,1)S(1)} %iota_compare_fusion), kind=kLoop, calls=%fused_computation.9 | loop fusion | flops 12578816 | bytes 12621824 | tf_op jit(solution)/shard_map/reduce_sum | solution.py:51
  49.1 0.6 fusion.4
  49.8 7.3 %fusion.3 = f32[8,2,8,32,128]{4,3,2,1,0:T(8,128)S(1)} fusion(bf16[8,768,2,128,1]{1,3,4,2,0:T(8,128)(2,1)} %bitcast.79, f32[8,2,768,32,8]{2,3,4,1,0:T(8,128)} %copy-done.1, f32[8,2,8,32]{3,2,1,0:T(8,128)S(1)} %add.48, f32[8,2,8,32]{3,2,1,0:T(8,128)S(1)} %max.9, pred[8,768]{1,0:T(8,128)(4,1)S(1)} %iota_compare_fusion), kind=kOutput, calls=%fused_computation.10 | convolution fusion | flops 821035008 | bytes 17864704 | tf_op jit(solution)/shard_map/ckgtp,cpkd->ctkgd/dot_general | solution.py:54
  57.1 0.7 fusion.5
  57.8 0.4 copy.90
  58.2 0.5 convert_element_type.34
  58.7 10.1 %fusion.30 = f32[256,4096]{1,0:T(8,128)} fusion(bf16[256,2048]{1,0:T(8,128)(2,1)S(1)} %convert_element_type.34, bf16[2048,4096]{1,0:T(8,128)(2,1)} %param.14), kind=kOutput, calls=%fused_computation.72 | convolution fusion | flops 4294967296 | bytes 22020096 | tf_op jit(solution)/shard_map/dot_general | solution.py:63
  68.8 0.6 copy-done.8
  69.5 26.6 %all-to-all-done = bf16[4,2,768,256]{3,1,0,2:T(2,128)(2,1)} async-done(((bf16[4,2,768,256]{3,1,0,2:T(2,128)(2,1)}), bf16[4,2,768,256]{3,1,0,2:T(2,128)(2,1)}, u32[]{:S(2)}, u32[]{:S(2)}) %all-to-all-start) | async-done | bytes 3145760 | tf_op jit(solution)/shard_map/all_to_all | solution.py:78
  96.1 2.5 %copy.92 = bf16[4,2,768,256]{3,2,1,0:T(8,128)(2,1)S(1)} copy(bf16[4,2,768,256]{3,1,0,2:T(2,128)(2,1)} %all-to-all-done) | data formatting | bytes 6291456 | tf_op jit(solution)/shard_map/all_to_all | solution.py:78
  98.6 1.9 copy.93
  100.6 2.6 %gather_fusion.2 = bf16[32,2,96,256]{3,2,1,0:T(8,128)(2,1)S(1)} fusion(bf16[32,2,96,256]{3,2,1,0:T(8,128)(2,1)} %bitcast.74, s32[1024]{0:T(1024)S(1)} %pad_clamp_fusion), kind=kCustom, calls=%fused_computation.2 | custom fusion | bytes 6291584 | tf_op jit(solution)/shard_map/jit(_take)/gather | solution.py:79
  103.2 2.0 %broadcast_select_fusion.1 = bf16[32,2,96,256]{3,2,1,0:T(8,128)(2,1)} fusion(bf16[32,2,96,256]{3,2,1,0:T(8,128)(2,1)S(1)} %gather_fusion.2, pred[32]{0:T(512)(128)(4,1)S(1)} %get-tuple-element.6), kind=kLoop, calls=%fused_computation.13 | loop fusion | flops 1572864 | bytes 6291488 | tf_op jit(solution)/shard_map/jit(_take)/select_n | solution.py:79
  105.3 3.8 %all-to-all-start.1 = ((bf16[32,2,96,256]{3,2,1,0:T(8,128)(2,1)}), bf16[32,2,96,256]{3,2,1,0:T(8,128)(2,1)S(1)}, u32[]{:S(2)}, u32[]{:S(2)}) async-start(bf16[32,2,96,256]{3,2,1,0:T(8,128)(2,1)} %broadcast_select_fusion.1), calls=%async_computation.2 | async-start | bytes 6291456 | tf_op jit(solution)/shard_map/all_to_all | solution.py:80
  109.1 0.1 compare_select_fusion.3
  109.2 0.6 gather_fusion
  109.9 0.1 iota_compare_fusion.3
  110.0 4.8 %reduce-scatter.2.cloned.1.call-done = f32[256,1024]{1,0:T(8,128)} async-done(((f32[256,4096]{1,0:T(8,128)}), f32[256,1024]{1,0:T(8,128)}) %reduce-scatter.2.cloned.1.call-update) | async-done | bytes 1048592 | tf_op jit(solution)/shard_map/reduce_scatter | solution.py:64
  114.7 2.1 %convert_element_type.35 = bf16[256,1024]{1,0:T(8,128)(2,1)} convert(f32[256,1024]{1,0:T(8,128)} %reduce-scatter.2.cloned.1.call-done) | non-fusion elementwise | flops 262144 | bytes 1572864 | tf_op jit(solution)/shard_map/convert_element_type | solution.py:64
  116.8 63.1 %all-to-all-done.1 = bf16[32,2,96,256]{3,2,1,0:T(8,128)(2,1)S(1)} async-done(((bf16[32,2,96,256]{3,2,1,0:T(8,128)(2,1)}), bf16[32,2,96,256]{3,2,1,0:T(8,128)(2,1)S(1)}, u32[]{:S(2)}, u32[]{:S(2)}) %all-to-all-start.1) | async-done | bytes 3145760 | tf_op jit(solution)/shard_map/all_to_all | solution.py:80
  179.9 0.3 copy.94
  180.2 0.4 copy-done.5
  180.6 0.8 bitcast_select_fusion
  181.4 0.2 fusion.26
  181.7 1.4 copy-done.2
  183.1 1.6 copy.97
  184.7 0.7 copy.95
  185.4 0.3 fusion.9
  185.7 0.2 fusion.29
  185.9 2.0 %fusion.10 = bf16[1,4,16,128]{3,2,1,0:T(8,128)(2,1)S(1)} fusion(bf16[4,768,2,128]{1,3,2,0:T(8,128)(2,1)} %bitcast.80, f32[4,2,8]{2,1,0:T(2,128)S(1)} %fusion.29, f32[4,2,8,768]{3,2,1,0:T(8,128)S(1)} %fusion.9), kind=kOutput, calls=%fused_computation.26 | convolution fusion | flops 12739391 | bytes 1786112 | tf_op jit(solution)/shard_map/skgp,spkd->skgd/dot_general | solution.py:98
  187.9 0.6 copy.138
  (34 shorter events, 0.4 us)
Async XLA Ops:
  7.2 102.0 %copy-start = (s32[64]{0:T(128)S(1)}, s32[64]{0:T(128)}, u32[]{:S(2)}) copy-start(s32[64]{0:T(128)} %param.16) | copy-start | bytes 772
  7.9 1.0 copy-start.7
  8.7 0.5 copy-start.9
  18.0 78.1 %all-to-all-start = ((bf16[4,2,768,256]{3,1,0,2:T(2,128)(2,1)}), bf16[4,2,768,256]{3,1,0,2:T(2,128)(2,1)}, u32[]{:S(2)}, u32[]{:S(2)}) async-start(bf16[4,2,768,256]{3,1,0,2:T(2,128)(2,1)} %copy.91), calls=%async_computation.1 | async-start | bytes 6291456 | tf_op jit(solution)/shard_map/all_to_all | solution.py:78
  25.3 89.4 %reduce-scatter.2.cloned.1.call-start = ((), (), s32[]{:S(2)}) async-start(), calls=%async_computation.3 | async-start | bytes 5242880 | tf_op jit(solution)/shard_map/reduce_scatter | solution.py:64
  30.6 2.8 %copy-start.11 = (s32[8]{0:T(128)S(1)}, s32[8]{0:T(128)}, u32[]{:S(2)}) copy-start(s32[8]{0:T(128)} %param.13) | copy-start | bytes 100
  40.1 3.7 %copy-start.3 = (bf16[32,8,16,128]{3,2,1,0:T(8,128)(2,1)S(1)}, bf16[32,8,16,128]{3,2,1,0:T(8,128)(2,1)}, u32[]{:S(2)}) copy-start(bf16[32,8,16,128]{3,2,1,0:T(8,128)(2,1)} %copy.116) | copy-start | bytes 3145732
  43.8 5.3 %copy-start.1 = (f32[8,2,768,32,8]{2,3,4,1,0:T(8,128)}, f32[8,2,768,32,8]{2,3,4,1,0:T(8,128)S(1)}, u32[]{:S(2)}) copy-start(f32[8,2,768,32,8]{2,3,4,1,0:T(8,128)S(1)} %get-tuple-element.19) | copy-start | bytes 37748740
  68.8 0.7 copy-start.8
  68.8 0.7 copy-start.10
  105.3 3.8 %copy-start.6 = (s32[32]{0:T(128)S(1)}, s32[32]{0:T(128)}, u32[]{:S(2)}) copy-start(s32[32]{0:T(128)} %param.17) | copy-start | bytes 388
  105.3 74.7 %all-to-all-start.1 = ((bf16[32,2,96,256]{3,2,1,0:T(8,128)(2,1)}), bf16[32,2,96,256]{3,2,1,0:T(8,128)(2,1)S(1)}, u32[]{:S(2)}, u32[]{:S(2)}) async-start(bf16[32,2,96,256]{3,2,1,0:T(8,128)(2,1)} %broadcast_select_fusion.1), calls=%async_computation.2 | async-start | bytes 6291456 | tf_op jit(solution)/shard_map/all_to_all | solution.py:80
  179.9 0.7 copy-start.5
  181.4 1.7 copy-start.2
  183.1 2.3 %copy-start.4 = (bf16[4,2048]{1,0:T(4,128)(2,1)S(1)}, bf16[4,2048]{1,0:T(4,128)(2,1)}, u32[]{:S(2)}) copy-start(bf16[4,2048]{1,0:T(4,128)(2,1)} %param.18) | copy-start | bytes 49156
Sparse Core Ops, SparseCore 0:
  69.0 45.6 reduce-scatter.1
